TPU v7x, 32 devices: a whole 2x2x4 slice. The times are simulated.
32 devices in a mesh: sec: 4 (over y, x), dev: 8 (over z, core).
Axes of the slice: x: 2, y: 2, z: 4, core: 2. Of those that a mesh axis runs over, the one named last changes fastest.
Arguments:
- tile_inverse: bfloat16 [32, 4, 512, 512], P(('sec', 'dev'))
- link_coupling: bfloat16 [32, 512, 2048], P(('sec', 'dev')), may hold values from -0.125 to 0.125
- link_panels: int32 [32, 4], P(('sec', 'dev')), may hold values from 0 to 63, all different within a row
- leaf_rhs: bfloat16 [32, 48, 2048], P(('sec', 'dev')), may hold values from -6 to 6
- leaf_scale: float32 [32, 2048], P(('sec', 'dev')), may hold values from 0.1 to 0.5
- link_scale: float32 [8192], replicated, may hold values from 0.2 to 2
- link_inverse: bfloat16 [8192, 8192], P('sec', 'dev'), as said below
Outputs:
- leaf_step: bfloat16 [32, 48, 2048], P(('sec', 'dev'))
- link_step: bfloat16 [48, 8192], P(None, 'dev')
Inputs may be any that keep to these rules, and one draw needn't show every extreme that they name: `link_panels`: the 4 panels of one block are different. link_inverse is symmetric.
All inputs are finite; a program needn't handle non-finite values.
Results may differ from a plain program's by a relative error of at most 0.02.
Values may be sent and summed in bfloat16 or wider, within the bound.
A program may use at most 64 MiB of HBM per device.

v0:
```python
import jax
import jax.numpy as jnp
from jax import lax
from jax.sharding import PartitionSpec as P

LINK = 8192
PANEL = 128
PB = 4
SOLVES = 5


def apply_tiles(tile_inv, vectors):
    columns = vectors.shape[0]
    blocked = vectors.reshape(columns, tile_inv.shape[0], tile_inv.shape[1])
    result = jnp.einsum("tab,ctb->cta", tile_inv, blocked, preferred_element_type=jnp.float32)
    return result.reshape(columns, -1)


def per_device(
    tile_inverse, link_coupling, link_panels, leaf_rhs, leaf_scale, link_scale, link_inverse
):
    tile_inv = tile_inverse[0]
    coupling = link_coupling[0]
    leaf_gain = leaf_scale[0]
    own_panels = link_panels[0]
    panel_count = LINK // PANEL
    matches = own_panels[:, None] == jnp.arange(panel_count, dtype=jnp.int32)[None, :]
    selector = matches.astype(jnp.bfloat16)
    spreader = matches.astype(jnp.float32)
    total_cols = leaf_rhs.shape[1]
    halves = 1
    half_cols = total_cols // halves
    previous = jnp.zeros((total_cols, leaf_rhs.shape[2]), jnp.bfloat16)
    linking_all = jnp.zeros((total_cols, LINK), jnp.bfloat16)
    for solve_index in range(SOLVES):
        rhs_part = leaf_rhs[0, 0:half_cols]
        corrected = rhs_part.astype(jnp.float32) - leaf_gain[None, :] * previous.astype(jnp.float32)
        corrected = corrected.astype(jnp.bfloat16)
        link_side = -link_scale[None, :] * linking_all.astype(jnp.float32)
        columns = corrected.shape[0]
        solved = apply_tiles(tile_inv, corrected).astype(jnp.bfloat16)
        touched = jnp.einsum("cn,rn->cr", solved, coupling, preferred_element_type=jnp.float32)
        touched_blocks = touched.reshape(columns, PB, PANEL)
        spread = jnp.einsum("csr,sq->cqr", touched_blocks, spreader).reshape(columns, LINK)
        section = lax.psum_scatter(
            spread.astype(jnp.bfloat16), "sec", scatter_dimension=1, tiled=True
        ).astype(jnp.float32)
        summed = lax.psum(section, "dev")
        one_slab_width = summed.shape[1]
        own_slab = lax.dynamic_slice_in_dim(
            link_side, lax.axis_index("sec") * one_slab_width, one_slab_width, 1
        )
        link_rhs = (own_slab - summed).astype(jnp.bfloat16)
        partial_value = jnp.dot(link_rhs, link_inverse, preferred_element_type=jnp.float32)
        own_part = lax.psum(partial_value, "sec").astype(jnp.bfloat16)
        linking = lax.all_gather(own_part, "dev", axis=1, tiled=True)
        picked = jnp.einsum(
            "cqr,sq->csr",
            linking.reshape(columns, panel_count, PANEL),
            selector,
            preferred_element_type=jnp.float32,
        )
        picked = picked.reshape(columns, PB * PANEL).astype(jnp.bfloat16)
        pushed = jnp.dot(picked, coupling, preferred_element_type=jnp.float32)
        reduced = (corrected.astype(jnp.float32) - pushed).astype(jnp.bfloat16)
        leaf_new = apply_tiles(tile_inv, reduced).astype(jnp.bfloat16)
        previous = leaf_new
        linking_all = linking
    slab_width = LINK // lax.axis_size("dev")
    link_out = lax.dynamic_slice_in_dim(
        linking_all, lax.axis_index("dev") * slab_width, slab_width, 1
    )
    return (previous[None], link_out)


def solution(mesh):
    in_specs = (
        P(("sec", "dev"), None, None, None),
        P(("sec", "dev"), None, None),
        P(("sec", "dev"), None),
        P(("sec", "dev"), None, None),
        P(("sec", "dev"), None),
        P(),
        P("sec", "dev"),
    )
    out_specs = (P(("sec", "dev"), None, None), P(None, "dev"))
    return jax.shard_map(
        per_device, mesh=mesh, in_specs=in_specs, out_specs=out_specs, check_vma=False
    )
```

profile of v0, /device:TPU:0, one launch (start us, length us, event | category | flops | bytes accessed | tf_op | source)
XLA Modules:
  0.0 550.5 jit_solution(4031400296671197560)
XLA Ops:
  10.4 2.3 fusion.87
  15.9 28.8 %reduce-scatter.6.cloned.1.call-done = bf16[48,2048]{1,0:T(8,128)(2,1)} async-done(((bf16[48,8192]{1,0:T(8,128)(2,1)}), bf16[48,2048]{1,0:T(8,128)(2,1)}) %reduce-scatter.6.cloned.1.call-update) | async-done | bytes 196624 | tf_op jit(solution)/shard_map/reduce_scatter | solution.py:45
  44.7 33.6 %all-reduce.10 = f32[48,2048]{1,0:T(8,128)S(1)} all-reduce(bf16[48,2048]{1,0:T(8,128)(2,1)} %reduce-scatter.6.cloned.1.call-done), channel_id=1, replica_groups=mesh['sec'=4,'dev'=8] {'dev'}, use_global_device_ids=true, to_apply=%region_1.0 | all-reduce | flops 98304 | bytes 589824 | tf_op jit(solution)/shard_map/psum | solution.py:48
  78.4 3.0 fusion.99
  81.4 19.2 %all-reduce.11 = bf16[48,1024]{1,0:T(8,128)(2,1)} all-reduce(f32[48,1024]{1,0:T(8,128)S(1)} %fusion.99), channel_id=1, replica_groups=mesh['sec'=4,'dev'=8] {'sec'}, use_global_device_ids=true, to_apply=%region_2.0 | all-reduce | flops 49152 | bytes 294912 | tf_op jit(solution)/shard_map/psum | solution.py:55
  100.6 15.9 %all_gather.15 = bf16[48,8192]{1,0:T(8,128)(2,1)S(1)} all-gather(bf16[48,1024]{1,0:T(8,128)(2,1)} %all-reduce.11), channel_id=1, replica_groups=mesh['sec'=4,'dev'=8] {'dev'}, dimensions={1}, use_global_device_ids=true | all-gather | bytes 884736 | tf_op jit(solution)/shard_map/all_gather | solution.py:56
  120.5 1.7 reshape.167
  125.8 1.8 copy.53
  127.6 21.8 %reduce-scatter.8.cloned.1.call-done = bf16[48,2048]{1,0:T(8,128)(2,1)} async-done(((bf16[48,8192]{1,0:T(8,128)(2,1)}), bf16[48,2048]{1,0:T(8,128)(2,1)}) %reduce-scatter.8.cloned.1.call-update) | async-done | bytes 196624 | tf_op jit(solution)/shard_map/reduce_scatter | solution.py:45
  149.4 34.2 %all-reduce.12 = f32[48,2048]{1,0:T(8,128)} all-reduce(bf16[48,2048]{1,0:T(8,128)(2,1)} %reduce-scatter.8.cloned.1.call-done), channel_id=1, replica_groups=mesh['sec'=4,'dev'=8] {'dev'}, use_global_device_ids=true, to_apply=%region_4.0 | all-reduce | flops 98304 | bytes 589824 | tf_op jit(solution)/shard_map/psum | solution.py:48
  183.6 3.8 fusion.100
  187.5 19.7 %all-reduce.13 = bf16[48,1024]{1,0:T(8,128)(2,1)} all-reduce(f32[48,1024]{1,0:T(8,128)} %fusion.100), channel_id=1, replica_groups=mesh['sec'=4,'dev'=8] {'sec'}, use_global_device_ids=true, to_apply=%region_5.0 | all-reduce | flops 49152 | bytes 294912 | tf_op jit(solution)/shard_map/psum | solution.py:55
  207.2 16.2 %all_gather.16 = bf16[48,8192]{1,0:T(8,128)(2,1)S(1)} all-gather(bf16[48,1024]{1,0:T(8,128)(2,1)} %all-reduce.13), channel_id=1, replica_groups=mesh['sec'=4,'dev'=8] {'dev'}, dimensions={1}, use_global_device_ids=true | all-gather | bytes 884736 | tf_op jit(solution)/shard_map/all_gather | solution.py:56
  227.5 1.7 reshape.168
  232.9 1.8 copy.54
  234.7 21.9 %reduce-scatter.10.cloned.1.call-done = bf16[48,2048]{1,0:T(8,128)(2,1)} async-done(((bf16[48,8192]{1,0:T(8,128)(2,1)}), bf16[48,2048]{1,0:T(8,128)(2,1)}) %reduce-scatter.10.cloned.1.call-update) | async-done | bytes 196624 | tf_op jit(solution)/shard_map/reduce_scatter | solution.py:45
  256.5 34.2 %all-reduce.14 = f32[48,2048]{1,0:T(8,128)} all-reduce(bf16[48,2048]{1,0:T(8,128)(2,1)} %reduce-scatter.10.cloned.1.call-done), channel_id=1, replica_groups=mesh['sec'=4,'dev'=8] {'dev'}, use_global_device_ids=true, to_apply=%region_7.0 | all-reduce | flops 98304 | bytes 589824 | tf_op jit(solution)/shard_map/psum | solution.py:48
  290.7 3.8 fusion.101
  294.6 19.7 %all-reduce.15 = bf16[48,1024]{1,0:T(8,128)(2,1)} all-reduce(f32[48,1024]{1,0:T(8,128)} %fusion.101), channel_id=1, replica_groups=mesh['sec'=4,'dev'=8] {'sec'}, use_global_device_ids=true, to_apply=%region_8.0 | all-reduce | flops 49152 | bytes 294912 | tf_op jit(solution)/shard_map/psum | solution.py:55
  314.3 16.0 %all_gather.17 = bf16[48,8192]{1,0:T(8,128)(2,1)S(1)} all-gather(bf16[48,1024]{1,0:T(8,128)(2,1)} %all-reduce.15), channel_id=1, replica_groups=mesh['sec'=4,'dev'=8] {'dev'}, dimensions={1}, use_global_device_ids=true | all-gather | bytes 884736 | tf_op jit(solution)/shard_map/all_gather | solution.py:56
  334.4 1.7 reshape.169
  339.8 1.8 copy.55
  341.6 21.9 %reduce-scatter.12.cloned.1.call-done = bf16[48,2048]{1,0:T(8,128)(2,1)} async-done(((bf16[48,8192]{1,0:T(8,128)(2,1)}), bf16[48,2048]{1,0:T(8,128)(2,1)}) %reduce-scatter.12.cloned.1.call-update) | async-done | bytes 196624 | tf_op jit(solution)/shard_map/reduce_scatter | solution.py:45
  363.4 34.2 %all-reduce.16 = f32[48,2048]{1,0:T(8,128)} all-reduce(bf16[48,2048]{1,0:T(8,128)(2,1)} %reduce-scatter.12.cloned.1.call-done), channel_id=1, replica_groups=mesh['sec'=4,'dev'=8] {'dev'}, use_global_device_ids=true, to_apply=%region_10.0 | all-reduce | flops 98304 | bytes 589824 | tf_op jit(solution)/shard_map/psum | solution.py:48
  397.7 3.8 fusion.102
  401.5 19.7 %all-reduce.17 = bf16[48,1024]{1,0:T(8,128)(2,1)} all-reduce(f32[48,1024]{1,0:T(8,128)} %fusion.102), channel_id=1, replica_groups=mesh['sec'=4,'dev'=8] {'sec'}, use_global_device_ids=true, to_apply=%region_11.0 | all-reduce | flops 49152 | bytes 294912 | tf_op jit(solution)/shard_map/psum | solution.py:55
  421.2 16.2 %all_gather.18 = bf16[48,8192]{1,0:T(8,128)(2,1)S(1)} all-gather(bf16[48,1024]{1,0:T(8,128)(2,1)} %all-reduce.17), channel_id=1, replica_groups=mesh['sec'=4,'dev'=8] {'dev'}, dimensions={1}, use_global_device_ids=true | all-gather | bytes 884736 | tf_op jit(solution)/shard_map/all_gather | solution.py:56
  444.5 22.9 %reduce-scatter.14.cloned.1.call-done = bf16[48,2048]{1,0:T(8,128)(2,1)} async-done(((bf16[48,8192]{1,0:T(8,128)(2,1)}), bf16[48,2048]{1,0:T(8,128)(2,1)}) %reduce-scatter.14.cloned.1.call-update) | async-done | bytes 196624 | tf_op jit(solution)/shard_map/reduce_scatter | solution.py:45
  467.4 33.6 %all-reduce.18 = f32[48,2048]{1,0:T(8,128)S(1)} all-reduce(bf16[48,2048]{1,0:T(8,128)(2,1)} %reduce-scatter.14.cloned.1.call-done), channel_id=1, replica_groups=mesh['sec'=4,'dev'=8] {'dev'}, use_global_device_ids=true, to_apply=%region_13.0 | all-reduce | flops 98304 | bytes 589824 | tf_op jit(solution)/shard_map/psum | solution.py:48
  501.1 3.7 fusion.103
  504.8 19.3 %all-reduce.19 = bf16[48,1024]{1,0:T(8,128)(2,1)S(1)} all-reduce(f32[48,1024]{1,0:T(8,128)} %fusion.103), channel_id=1, replica_groups=mesh['sec'=4,'dev'=8] {'sec'}, use_global_device_ids=true, to_apply=%region_14.0 | all-reduce | flops 49152 | bytes 294912 | tf_op jit(solution)/shard_map/psum | solution.py:55
  524.1 15.7 %all_gather.19 = bf16[48,8192]{1,0:T(8,128)(2,1)S(1)} all-gather(bf16[48,1024]{1,0:T(8,128)(2,1)S(1)} %all-reduce.19), channel_id=1, replica_groups=mesh['sec'=4,'dev'=8] {'dev'}, dimensions={1}, use_global_device_ids=true | all-gather | bytes 884736 | tf_op jit(solution)/shard_map/all_gather | solution.py:56
  (106 shorter events, 40.1 us)
Async XLA Ops:
  7.2 5.9 %copy-start = (bf16[1,512,2048]{2,1,0:T(8,128)(2,1)S(1)}, bf16[1,512,2048]{2,1,0:T(8,128)(2,1)}, u32[]{:S(2)}) copy-start(bf16[1,512,2048]{2,1,0:T(8,128)(2,1)} %param.8) | copy-start | bytes 6291460
  7.2 37.6 %reduce-scatter.6.cloned.1.call-start = ((), (), s32[]{:S(2)}) async-start(), calls=%async_computation.5 | async-start | bytes 983040 | tf_op jit(solution)/shard_map/reduce_scatter | solution.py:45
  12.8 1.1 copy-start.17
  13.8 2.0 copy-start.18
  13.9 2.0 copy-start.16
  15.8 133.6 %reduce-scatter.8.cloned.1.call-start = ((), (), s32[]{:S(2)}) async-start(), calls=%async_computation.6 | async-start | bytes 983040 | tf_op jit(solution)/shard_map/reduce_scatter | solution.py:45
  81.4 35.6 %copy-start.6 = (bf16[1,48,2048]{2,1,0:T(8,128)(2,1)S(1)}, bf16[1,48,2048]{2,1,0:T(8,128)(2,1)}, u32[]{:S(2)}) copy-start(bf16[1,48,2048]{2,1,0:T(8,128)(2,1)} %param.10) | copy-start | bytes 589828
  116.6 1.6 copy-start.1
  118.9 0.8 copy-start.9
  125.8 130.7 %reduce-scatter.10.cloned.1.call-start = ((), (), s32[]{:S(2)}) async-start(), calls=%async_computation.7 | async-start | bytes 983040 | tf_op jit(solution)/shard_map/reduce_scatter | solution.py:45
  207.2 16.7 %copy-start.13 = (f32[4,6,8,512]{3,2,0,1:T(8,128)S(1)}, f32[4,6,8,512]{3,2,0,1:T(8,128)}, u32[]{:S(2)}) copy-start(f32[4,6,8,512]{3,2,0,1:T(8,128)} %copy.53) | copy-start | bytes 1179652
  223.6 1.6 copy-start.2
  225.9 0.8 copy-start.10
  232.8 130.6 %reduce-scatter.12.cloned.1.call-start = ((), (), s32[]{:S(2)}) async-start(), calls=%async_computation.8 | async-start | bytes 983040 | tf_op jit(solution)/shard_map/reduce_scatter | solution.py:45
  314.2 16.5 %copy-start.14 = (f32[4,6,8,512]{3,2,0,1:T(8,128)S(1)}, f32[4,6,8,512]{3,2,0,1:T(8,128)}, u32[]{:S(2)}) copy-start(f32[4,6,8,512]{3,2,0,1:T(8,128)} %copy.54) | copy-start | bytes 1179652
  330.5 1.6 copy-start.3
  332.8 0.8 copy-start.11
  339.7 127.7 %reduce-scatter.14.cloned.1.call-start = ((), (), s32[]{:S(2)}) async-start(), calls=%async_computation.9 | async-start | bytes 983040 | tf_op jit(solution)/shard_map/reduce_scatter | solution.py:45
  421.2 16.7 %copy-start.15 = (f32[4,6,8,512]{3,2,0,1:T(8,128)S(1)}, f32[4,6,8,512]{3,2,0,1:T(8,128)}, u32[]{:S(2)}) copy-start(f32[4,6,8,512]{3,2,0,1:T(8,128)} %copy.55) | copy-start | bytes 1179652
  437.6 1.6 copy-start.4
  439.9 0.8 copy-start.7
  441.8 1.9 copy-start.8
  504.8 36.1 %copy-start.12 = (f32[4,6,8,512]{3,2,0,1:T(8,128)S(1)}, f32[4,6,8,512]{3,2,0,1:T(8,128)}, u32[]{:S(2)}) copy-start(f32[4,6,8,512]{3,2,0,1:T(8,128)} %copy.56) | copy-start | bytes 1179652
  540.6 1.6 copy-start.5
Sparse Core Ops, SparseCore 0:
  15.9 28.7 reduce-scatter.5
  125.9 23.4 reduce-scatter.7
  232.9 23.5 reduce-scatter.9
  339.8 23.5 reduce-scatter.11
  443.8 23.5 reduce-scatter.13
where the time goes:
time: 552 us; the launch traced here: 550 us
  blocking collectives  348 us (63%)
  waiting for transfers between devices  117 us (21%)
  matrix products  39.9 us (7%)
  local copies, waits for them, and re-layouts  29.7 us (5%)
  between operations  14.4 us (3%)
    psum x5, blocking collectives, per_device(): summed = lax.psum(section, 'dev')  170 us
    reduce_scatter x5, waiting for transfers between devices, per_device(): lax.psum_scatter(spread.astype(jnp.bfloat16), 'sec', scatter_dimension=1,...  117 us
    psum x5, blocking collectives, per_device(): own_part = lax.psum(partial_value, 'sec').astype(jnp.bfloat16)  97.6 us
    all_gather x5, blocking collectives, per_device(): linking = lax.all_gather(own_part, 'dev', axis=1, tiled=True)  80.1 us
    dot_general x5, matrix products, per_device(): jnp.dot(link_rhs, link_inverse, preferred_element_type=jnp.float32)  18.2 us
    unnamed x49, local copies, waits for them, and re-layouts  12.4 us
  transfers between devices with their start and end apart: 5, of which 5 were waited for; matrix products, arithmetic and copies ran while one was open for 1% of the time, Pallas kernels for 0%

commit v1 on v0

v1 whole, which is shorter than its diff:
```python
import functools

import jax
import jax.numpy as jnp
from jax import lax
from jax.experimental import pallas as pl
from jax.experimental.pallas import tpu as pltpu
from jax.sharding import PartitionSpec as P

SOLVES = 5
F32 = jnp.float32
BF16 = jnp.bfloat16


def nn(a, b):
    return lax.dot_general(a, b, (((1,), (0,)), ((), ())), preferred_element_type=F32)


def nt(a, b):
    return lax.dot_general(a, b, (((1,), (1,)), ((), ())), preferred_element_type=F32)


def kernel(
    n_sec, n_dev, per,
    panels_ref, slot_ref, tile_ref, coup_ref, rhs_ref, scale_ref, lscale_ref, linv_hbm,
    leaf_out, link_out,
    linv, slot_v, slot_s, tbuf, rsend, rrecv, hbuf, lsend, lrecv, link,
    mmat, qmat, kmat, kacc, base, solved, umat, picked, part,
    in_sem, slot_sem, slot_send, slot_recv,
    t_send, t_recv, r_send, r_recv, h_send, h_recv, l_send, l_recv,
    z_send, z_recv, g_send, g_recv, c_send, c_recv,
):
    s = lax.axis_index("sec")
    d = lax.axis_index("dev")
    n_z = n_dev // 2
    z = d // 2
    c = d % 2
    partner = z * 2 + (1 - c)
    pb = tbuf.shape[2] - 1
    tiles, tile = tile_ref.shape[0], tile_ref.shape[1]
    panel = tbuf.shape[4]
    per_sec = n_dev * per
    per_dev = n_sec * per

    def remote(src, dst, send, recv, target):
        return pltpu.make_async_remote_copy(
            src_ref=src, dst_ref=dst, send_sem=send, recv_sem=recv,
            device_id=target, device_id_type=pl.DeviceIdType.MESH,
        )

    linv_copy = pltpu.make_async_copy(linv_hbm, linv, in_sem)
    linv_copy.start()

    barrier = pltpu.get_barrier_semaphore()
    for j in range(1, n_dev):
        pl.semaphore_signal(barrier, inc=1, device_id={"dev": (d + j) % n_dev},
                            device_id_type=pl.DeviceIdType.MESH)
    for j in range(1, n_sec):
        pl.semaphore_signal(barrier, inc=1, device_id={"sec": (s + j) % n_sec},
                            device_id_type=pl.DeviceIdType.MESH)

    zero_panel = jnp.zeros(tbuf.shape[3:], BF16)
    for k in range(SOLVES):
        for i in range(n_dev):
            tbuf[k, i, pb] = zero_panel
    own_rhs = s * per_sec + d * per
    for j in range(per):
        link[0, own_rhs + j] = zero_panel
    slot_v[d] = slot_ref[...]
    first = None
    for t in range(tiles):
        cols = pl.ds(t * tile, tile)
        value = nt(rhs_ref[:, cols], tile_ref[t])
        solved[:, cols] = value
        term = nt(value.astype(BF16), coup_ref[:, cols])
        first = term if first is None else first + term
    base[...] = first
    for q in range(pb):
        tbuf[0, d, q] = first[:, q * panel:(q + 1) * panel].astype(BF16)

    pl.semaphore_wait(barrier, n_dev - 1 + n_sec - 1)

    slot_copies = []
    for j in range(1, n_dev):
        copy = remote(slot_v.at[d], slot_v.at[d], slot_send.at[j], slot_recv.at[j],
                      {"dev": (d + j) % n_dev})
        copy.start()
        slot_copies.append(copy)

    def solve(k, carry):
        sends = []

        t_copies = []
        for j in range(1, n_dev):
            mine = tbuf.at[k, d, pl.ds(0, pb)]
            copy = remote(mine, mine, t_send.at[j], t_recv.at[j], {"dev": (d + j) % n_dev})
            copy.start()
            t_copies.append(copy)
        sends += t_copies

        @pl.when(k == 0)
        def _():
            for t in range(tiles):
                cols = pl.ds(t * tile, tile)
                mmat[:, cols] = nn(coup_ref[:, cols], tile_ref[t]).astype(BF16)
                qmat[:, cols] = nt(coup_ref[:, cols], tile_ref[t]).astype(BF16)
            for copy in slot_copies:
                copy.wait()
            to_smem = pltpu.make_async_copy(slot_v, slot_s, slot_sem)
            to_smem.start()
            to_smem.wait()

        @pl.when(k > 0)
        def _():
            for t in range(tiles):
                cols = pl.ds(t * tile, tile)
                leaf = solved[:, cols] - nn(picked[...], qmat[:, cols])
                x = rhs_ref[:, cols].astype(F32) - scale_ref[:, cols] * leaf
                solved[:, cols] = nt(x.astype(BF16), tile_ref[t])

        for copy in t_copies:
            copy.wait_recv()
        for a in range(n_sec):
            for j in range(per):
                q = a * per_sec + d * per + j
                total = tbuf[k, 0, slot_s[0, 0, q]].astype(F32)
                for i in range(1, n_dev):
                    total = total + tbuf[k, i, slot_s[i, 0, q]].astype(F32)
                rsend[k, a, j] = total.astype(BF16)

        r_copies = []
        for j in range(1, n_sec):
            to = (s + j) % n_sec
            copy = remote(rsend.at[k, to], rrecv.at[k, s], r_send.at[j], r_recv.at[j], {"sec": to})
            copy.start()
            r_copies.append(copy)
        sends += r_copies
        rhs_part = []
        for j in range(per):
            prev = link[k, own_rhs + j].astype(F32)
            rhs_part.append(-lscale_ref[own_rhs + j] * prev - rsend[k, s, j].astype(F32))
        for copy in r_copies:
            copy.wait_recv()
        for j in range(per):
            total = rhs_part[j]
            for i in range(1, n_sec):
                total = total - rrecv[k, (s + i) % n_sec, j].astype(F32)
            hbuf[k, d, j] = total.astype(BF16)

        h_copies = []
        for j in range(1, n_dev):
            mine = hbuf.at[k, d]
            copy = remote(mine, mine, h_send.at[j], h_recv.at[j], {"dev": (d + j) % n_dev})
            copy.start()
            h_copies.append(copy)
        sends += h_copies

        @pl.when(k == 0)
        def _():
            linv_copy.wait()

        def multiply(owner):
            left = jnp.concatenate([hbuf[k, owner, j] for j in range(per)], axis=1)
            depth = per * panel
            rows = pl.ds(pl.multiple_of(owner * depth, depth), depth)
            return nn(left, linv[rows, :])

        part[...] = multiply(d)

        @pl.when(k < SOLVES - 1)
        def _():
            total = base[...]
            for t in range(tiles):
                cols = pl.ds(t * tile, tile)
                scaled = (scale_ref[:, cols] * solved[:, cols]).astype(BF16)
                total = total - nt(scaled, mmat[:, cols])
            umat[...] = total

        for j in range(1, n_dev):
            h_copies[j - 1].wait_recv()
            part[...] += multiply((d - j + n_dev) % n_dev)
        for q in range(per_dev):
            lsend[k, q] = part[:, q * panel:(q + 1) * panel].astype(BF16)

        l_copies = []
        for j in range(1, n_sec):
            to = (s + j) % n_sec
            copy = remote(lsend.at[k, pl.ds(to * per, per)], lrecv.at[k, s],
                          l_send.at[j], l_recv.at[j], {"sec": to})
            copy.start()
            l_copies.append(copy)
        sends += l_copies

        @pl.when(k == 0)
        def _():
            for t in range(tiles):
                cols = pl.ds(t * tile, tile)
                scaled = (scale_ref[:, cols] * qmat[:, cols].astype(F32)).astype(BF16)
                term = nt(scaled, mmat[:, cols])
                if t == 0:
                    kacc[...] = term
                else:
                    kacc[...] += term
            kmat[...] = kacc[...].astype(BF16)

        for copy in l_copies:
            copy.wait_recv()
        for j in range(per):
            total = part[:, pl.ds(pl.multiple_of((s * per + j) * panel, panel), panel)]
            for i in range(1, n_sec):
                total = total + lrecv[k, (s + i) % n_sec, j].astype(F32)
            link[k + 1, d * per_dev + s * per + j] = total.astype(BF16)

        def piece(owner, section):
            return link.at[k + 1, pl.ds(owner * per_dev + section * per, per)]

        z_copies = []
        for j in range(1, n_z):
            copy = remote(piece(d, s), piece(d, s), z_send.at[j], z_recv.at[j],
                          {"dev": ((z + j) % n_z) * 2 + c})
            copy.start()
            z_copies.append(copy)
        sends += z_copies
        g_copies = []
        for i in range(n_z):
            owner = ((z - i + n_z) % n_z) * 2 + c
            if i > 0:
                z_copies[i - 1].wait_recv()
            group = []
            for j in range(1, n_sec):
                copy = remote(piece(owner, s), piece(owner, s), g_send.at[i, j], g_recv.at[i, j],
                              {"sec": (s + j) % n_sec})
                copy.start()
                group.append(copy)
            g_copies.append(group)
            sends += group
        c_copies = []
        for i in range(n_z):
            owner = ((z - i + n_z) % n_z) * 2 + c
            for copy in g_copies[i]:
                copy.wait_recv()
            whole = link.at[k + 1, pl.ds(owner * per_dev, per_dev)]
            copy = remote(whole, whole, c_send.at[i], c_recv.at[i], {"dev": partner})
            copy.start()
            c_copies.append(copy)
        sends += c_copies
        for copy in c_copies:
            copy.wait_recv()

        for q in range(pb):
            picked[:, q * panel:(q + 1) * panel] = link[k + 1, panels_ref[0, q]]

        @pl.when(k < SOLVES - 1)
        def _():
            touched = umat[...] + nn(picked[...], kmat[...])
            for q in range(pb):
                tbuf[k + 1, d, q] = touched[:, q * panel:(q + 1) * panel].astype(BF16)

        for copy in sends:
            copy.wait_send()
        return carry

    lax.fori_loop(0, SOLVES, solve, 0)

    for t in range(tiles):
        cols = pl.ds(t * tile, tile)
        leaf_out[:, cols] = (solved[:, cols] - nn(picked[...], qmat[:, cols])).astype(BF16)
    for q in range(per_dev):
        link_out[:, q * panel:(q + 1) * panel] = link[SOLVES, d * per_dev + q]


def fused(n_sec, n_dev, per, tile_inverse, link_coupling, link_panels, leaf_rhs, leaf_scale,
          link_scale, link_inverse):
    pb = link_panels.shape[1]
    rows, nb = link_coupling.shape[1:]
    panel = rows // pb
    cols = leaf_rhs.shape[1]
    total_panels = link_scale.shape[0] // panel
    order = jnp.arange(128, dtype=jnp.int32)
    matches = link_panels[0][:, None] == order[None, :]
    slots = pb - jnp.sum(
        jnp.where(matches, pb - jnp.arange(pb, dtype=jnp.int32)[:, None], 0), axis=0,
        dtype=jnp.int32,
    )
    slots = jnp.broadcast_to(slots[None, :], (8, 128))
    per_dev = n_sec * per
    n_z = n_dev // 2
    vmem = pl.BlockSpec(memory_space=pltpu.VMEM)
    dma = pltpu.SemaphoreType.DMA
    leaf, link = pl.pallas_call(
        functools.partial(kernel, n_sec, n_dev, per),
        out_shape=(
            jax.ShapeDtypeStruct((cols, nb), BF16),
            jax.ShapeDtypeStruct((cols, per_dev * panel), BF16),
        ),
        in_specs=[pl.BlockSpec(memory_space=pltpu.SMEM)] + [vmem] * 6
        + [pl.BlockSpec(memory_space=pl.ANY)],
        out_specs=(vmem, vmem),
        scratch_shapes=[
            pltpu.VMEM(link_inverse.shape, BF16),
            pltpu.VMEM((n_dev, 8, 128), jnp.int32),
            pltpu.SMEM((n_dev, 8, 128), jnp.int32),
            pltpu.VMEM((SOLVES, n_dev, pb + 1, cols, panel), BF16),
            pltpu.VMEM((SOLVES, n_sec, per, cols, panel), BF16),
            pltpu.VMEM((SOLVES, n_sec, per, cols, panel), BF16),
            pltpu.VMEM((SOLVES, n_dev, per, cols, panel), BF16),
            pltpu.VMEM((SOLVES, per_dev, cols, panel), BF16),
            pltpu.VMEM((SOLVES, n_sec, per, cols, panel), BF16),
            pltpu.VMEM((SOLVES + 1, total_panels, cols, panel), BF16),
            pltpu.VMEM((rows, nb), BF16),
            pltpu.VMEM((rows, nb), BF16),
            pltpu.VMEM((rows, rows), BF16),
            pltpu.VMEM((rows, rows), F32),
            pltpu.VMEM((cols, rows), F32),
            pltpu.VMEM((cols, nb), F32),
            pltpu.VMEM((cols, rows), F32),
            pltpu.VMEM((cols, rows), BF16),
            pltpu.VMEM((cols, per_dev * panel), F32),
            dma, dma, dma((n_dev,)), dma((n_dev,)),
            dma((n_dev,)), dma((n_dev,)), dma((n_sec,)), dma((n_sec,)),
            dma((n_dev,)), dma((n_dev,)), dma((n_sec,)), dma((n_sec,)),
            dma((n_z,)), dma((n_z,)), dma((n_z, n_sec)), dma((n_z, n_sec)),
            dma((n_z,)), dma((n_z,)),
        ],
        compiler_params=pltpu.CompilerParams(
            collective_id=0, has_side_effects=True, vmem_limit_bytes=48 * 1024 * 1024
        ),
    )(
        link_panels, slots, tile_inverse[0], link_coupling[0], leaf_rhs[0], leaf_scale,
        link_scale.reshape(total_panels, 1, panel), link_inverse,
    )
    return leaf[None], link


def apply_tiles(tile_inv, vectors):
    columns = vectors.shape[0]
    blocked = vectors.reshape(columns, tile_inv.shape[0], tile_inv.shape[1])
    result = jnp.einsum("tab,ctb->cta", tile_inv, blocked, preferred_element_type=F32)
    return result.reshape(columns, -1)


def plain(tile_inverse, link_coupling, link_panels, leaf_rhs, leaf_scale, link_scale, link_inverse):
    tile_inv, coupling, leaf_gain = tile_inverse[0], link_coupling[0], leaf_scale[0]
    own_panels = link_panels[0]
    pb = own_panels.shape[0]
    panel = coupling.shape[0] // pb
    link_size = link_scale.shape[0]
    panel_count = link_size // panel
    matches = own_panels[:, None] == jnp.arange(panel_count, dtype=jnp.int32)[None, :]
    selector = matches.astype(BF16)
    spreader = matches.astype(F32)
    columns = leaf_rhs.shape[1]
    previous = jnp.zeros(leaf_rhs.shape[1:], BF16)
    linking = jnp.zeros((columns, link_size), BF16)
    for solve_index in range(SOLVES):
        corrected = leaf_rhs[0].astype(F32) - leaf_gain[None, :] * previous.astype(F32)
        corrected = corrected.astype(BF16)
        link_side = -link_scale[None, :] * linking.astype(F32)
        solved = apply_tiles(tile_inv, corrected).astype(BF16)
        touched = jnp.einsum("cn,rn->cr", solved, coupling, preferred_element_type=F32)
        touched = touched.reshape(columns, pb, panel)
        spread = jnp.einsum("csr,sq->cqr", touched, spreader).reshape(columns, link_size)
        section = lax.psum_scatter(
            spread.astype(BF16), "sec", scatter_dimension=1, tiled=True
        ).astype(F32)
        summed = lax.psum(section, "dev")
        width = summed.shape[1]
        own_slab = lax.dynamic_slice_in_dim(link_side, lax.axis_index("sec") * width, width, 1)
        link_rhs = (own_slab - summed).astype(BF16)
        partial_value = jnp.dot(link_rhs, link_inverse, preferred_element_type=F32)
        own_part = lax.psum(partial_value, "sec").astype(BF16)
        linking = lax.all_gather(own_part, "dev", axis=1, tiled=True)
        picked = jnp.einsum(
            "cqr,sq->csr", linking.reshape(columns, panel_count, panel), selector,
            preferred_element_type=F32,
        )
        picked = picked.reshape(columns, pb * panel).astype(BF16)
        pushed = jnp.dot(picked, coupling, preferred_element_type=F32)
        reduced = (corrected.astype(F32) - pushed).astype(BF16)
        previous = apply_tiles(tile_inv, reduced).astype(BF16)
    width = link_size // lax.axis_size("dev")
    link_out = lax.dynamic_slice_in_dim(linking, lax.axis_index("dev") * width, width, 1)
    return previous[None], link_out


def per_device(n_sec, n_dev, *args):
    link_coupling, link_panels, link_scale = args[1], args[2], args[5]
    panel = link_coupling.shape[1] // link_panels.shape[1]
    panels = link_scale.shape[0] // panel
    fits = n_dev % 2 == 0 and panels % (n_sec * n_dev) == 0 and panels <= 128
    if fits and n_sec > 1 and link_coupling.shape[0] == 1:
        return fused(n_sec, n_dev, panels // (n_sec * n_dev), *args)
    return plain(*args)


def solution(mesh):
    in_specs = (
        P(("sec", "dev"), None, None, None),
        P(("sec", "dev"), None, None),
        P(("sec", "dev"), None),
        P(("sec", "dev"), None, None),
        P(("sec", "dev"), None),
        P(),
        P("sec", "dev"),
    )
    out_specs = (P(("sec", "dev"), None, None), P(None, "dev"))
    body = functools.partial(per_device, mesh.shape["sec"], mesh.shape["dev"])
    return jax.shard_map(
        body, mesh=mesh, in_specs=in_specs, out_specs=out_specs, check_vma=False
    )
```

time: 552 us -> 175 us (0.32)
  blocking collectives: 348 us -> 0 us
  Pallas kernels: 0 us -> 166 us
  waiting for transfers between devices: 117 us -> 0 us
  matrix products: 39.9 us -> 0 us
  local copies, waits for them, and re-layouts: 29.7 us -> 7.54 us
  between operations: 14.4 us -> 0.66 us
    psum x10 -> x0, blocking collectives: 267 us -> none  [the longest x5 170 us: per_device(): summed = lax.psum(section, 'dev')]
    pallas_call x0 -> x1, Pallas kernels: none -> 166 us  [fused(): pl.pallas_call(functools.partial(kernel, n_sec, n_dev, per), out_shape=(j...]
    reduce_scatter x5 -> x0, waiting for transfers between devices: 117 us -> none  [per_device(): lax.psum_scatter(spread.astype(jnp.bfloat16), 'sec', scatter_dimension=1,...]
    all_gather x5 -> x0, blocking collectives: 80.1 us -> none  [per_device(): linking = lax.all_gather(own_part, 'dev', axis=1, tiled=True)]
    dot_general x35 -> x0, matrix products: 39.9 us -> none  [the longest x5 18.2 us: per_device(): jnp.dot(link_rhs, link_inverse, preferred_element_type=jnp.float32)]
    convert_element_type x17 -> x0, local copies, waits for them, and re-layouts: 16.6 us -> none  [the longest x10 8.23 us: per_device(): solved = apply_tiles(tile_inv, corrected).astype(jnp.bfloat16)]
    unnamed x49 -> x14, local copies, waits for them, and re-layouts: 12.4 us -> 7.53 us
  transfers between devices with their start and end apart: 5 -> 0, of which waited for: 5 -> 0; matrix products, arithmetic and copies ran while one was open for 1% -> 0% of each run, Pallas kernels for 0% -> 0%
where the time goes in v1:
time: 175 us
  Pallas kernels  166 us (95%)
  local copies, waits for them, and re-layouts  7.54 us (4%)
    pallas_call x1, Pallas kernels, fused(): pl.pallas_call(functools.partial(kernel, n_sec, n_dev, per), out_shape=(j...  166 us
    unnamed x14, local copies, waits for them, and re-layouts  7.53 us

profile of v1, /device:TPU:0, one launch (start us, length us, event | category | flops | bytes accessed | tf_op | source)
XLA Modules:
  0.0 174.9 jit_solution(1798830380293208731)
XLA Ops:
  0.6 0.7 select_reduce_fusion
  1.4 0.0 copy-start
  1.4 1.6 copy-done
  3.0 0.0 copy-start.1
  3.0 1.6 copy-done.1
  4.6 0.0 copy-start.2
  4.6 0.9 copy-done.2
  5.5 0.0 copy-start.3
  5.5 0.8 copy-done.3
  6.3 0.0 copy-start.4
  6.3 0.7 copy-done.4
  7.0 0.0 copy-start.5
  7.0 0.7 copy-done.5
  7.6 165.9 %shard_map.86 = (bf16[48,2048]{1,0:T(8,128)(2,1)S(1)}, bf16[48,1024]{1,0:T(8,128)(2,1)S(1)}) custom-call(s32[1,4]{1,0:T(1,128)S(1)} %copy-done.5, s32[8,128]{1,0:T(8,128)S(1)} %broadcast_in_dim.25.slot_ref, bf16[4,512,512]{2,1,0:T(8,128)(2,1)S(1)} %bitcast.6, bf16[512,2048]{1,0:T(8,128)(2,1)S(1)} %bitcast.7, bf16[48,2048]{1,0:T(8,128)(2,1)S(1)} %bitcast.9, ...), custom_call_target="tpu_custom_call" | custom-call | tf_op jit(solution)/shard_map/pallas_call | solution.py:290
  173.6 0.7 copy.11
  174.2 0.6 copy.12
  (3 shorter events, 0.0 us)
Async XLA Ops:
  1.4 1.6 copy-start
  3.0 1.6 copy-start.1
  4.6 0.9 copy-start.2
  5.5 0.8 copy-start.3
  6.3 0.7 copy-start.4
  7.0 0.7 copy-start.5

commit v2 on v1

v2 whole, which is shorter than its diff:
```python
import functools

import jax
import jax.numpy as jnp
from jax import lax
from jax.experimental import pallas as pl
from jax.experimental.pallas import tpu as pltpu
from jax.sharding import PartitionSpec as P

SOLVES = 5
F32 = jnp.float32
BF16 = jnp.bfloat16


def nn(a, b):
    return lax.dot_general(a, b, (((1,), (0,)), ((), ())), preferred_element_type=F32)


def nt(a, b):
    return lax.dot_general(a, b, (((1,), (1,)), ((), ())), preferred_element_type=F32)


PER_GROUP = 7
SEMS = 18


def kernel(n_sec, n_dev, per, groups, *refs):
    (panels_ref, tile_hbm, coup_hbm, rhs_hbm, scale_hbm, lscale_hbm, linv_hbm,
     leaf_out, link_out,
     tile_ref, coup_ref, rhs_ref, scale_ref, lscale_ref, linv, slot_v, slot_s,
     mmat, qmat, kmat, kacc, base, solved, umat, picked, part,
     in_sem, slot_sem, slot_send, slot_recv) = refs[:30]
    rest = refs[30:]
    span = PER_GROUP + SEMS
    buffers = [rest[g * span:g * span + PER_GROUP] for g in range(len(groups))]
    sems = [rest[g * span + PER_GROUP:(g + 1) * span] for g in range(len(groups))]
    n_groups = range(len(groups))
    s = lax.axis_index("sec")
    d = lax.axis_index("dev")
    n_z = n_dev // 2
    z = d // 2
    c = d % 2
    partner = z * 2 + (1 - c)
    pb = panels_ref.shape[1]
    tiles, tile = tile_ref.shape[0], tile_ref.shape[1]
    panel = coup_ref.shape[0] // pb
    per_sec = n_dev * per
    per_dev = n_sec * per
    own_rhs = s * per_sec + d * per

    def remote(src, send, recv, target, dst=None):
        return pltpu.make_async_remote_copy(
            src_ref=src, dst_ref=src if dst is None else dst, send_sem=send, recv_sem=recv,
            device_id=target, device_id_type=pl.DeviceIdType.MESH,
        )

    def started(copies):
        for copy in copies:
            copy.start()
        return copies

    def on_z(j, core):
        return ((z - j + n_z) % n_z) * 2 + core

    def rows(g):
        return pl.ds(groups[g][0], groups[g][1])

    loads = []

    def load(src, dst):
        copy = pltpu.make_async_copy(src, dst, in_sem.at[len(loads)])
        copy.start()
        loads.append(copy)
        return copy

    rhs_load = load(rhs_hbm, rhs_ref)
    coup_load = load(coup_hbm, coup_ref)
    tile_loads = [load(tile_hbm.at[t], tile_ref.at[t]) for t in range(tiles)]
    scale_load = load(scale_hbm, scale_ref)
    lscale_load = load(lscale_hbm, lscale_ref)
    linv_load = load(linv_hbm, linv)

    barrier = pltpu.get_barrier_semaphore()
    for j in range(1, n_dev):
        pl.semaphore_signal(barrier, inc=1, device_id={"dev": (d + j) % n_dev},
                            device_id_type=pl.DeviceIdType.MESH)
    for j in range(1, n_sec):
        pl.semaphore_signal(barrier, inc=1, device_id={"sec": (s + j) % n_sec},
                            device_id_type=pl.DeviceIdType.MESH)

    for g in n_groups:
        tbuf, link = buffers[g][0], buffers[g][6]
        zero_panel = jnp.zeros(tbuf.shape[3:], BF16)
        for k in range(SOLVES):
            for i in range(n_dev):
                tbuf[k, i, pb] = zero_panel
        for j in range(per):
            link[0, own_rhs + j] = zero_panel
    lane = lax.broadcasted_iota(jnp.int32, slot_v.shape[1:], 1)
    slots = jnp.full(slot_v.shape[1:], pb, jnp.int32)
    for q in range(pb):
        slots = jnp.where(lane == panels_ref[0, q], q, slots)
    slot_v[d] = slots

    rhs_load.wait()
    first = None
    for t in range(tiles):
        cols = pl.ds(t * tile, tile)
        tile_loads[t].wait()
        value = nt(rhs_ref[:, cols], tile_ref[t])
        solved[:, cols] = value
        if t == 0:
            coup_load.wait()
        term = nt(value.astype(BF16), coup_ref[:, cols])
        first = term if first is None else first + term
    base[...] = first

    pl.semaphore_wait(barrier, n_dev - 1 + n_sec - 1)

    slot_copies = started([
        remote(slot_v.at[d], slot_send.at[j], slot_recv.at[j], {"dev": (d + j) % n_dev})
        for j in range(1, n_dev)
    ])

    def along_z(ref, send, recv):
        return [remote(ref, send.at[j], recv.at[j], {"dev": ((z + j) % n_z) * 2 + c})
                for j in range(1, n_z)]

    def to_core(ref, send, recv, j):
        return remote(ref, send.at[j], recv.at[j], {"dev": partner})

    def touched_first(g, k):
        mine = buffers[g][0].at[k, d, pl.ds(0, pb)]
        return (along_z(mine, sems[g][0], sems[g][1])
                + [to_core(mine, sems[g][2], sems[g][3], 0)])

    def store_touched(g, k, value):
        for q in range(pb):
            buffers[g][0][k, d, q] = value[:, q * panel:(q + 1) * panel].astype(BF16)
        started(touched_first(g, k))

    for g in n_groups:
        store_touched(g, 0, base[rows(g), :])
    scale_load.wait()
    lscale_load.wait()

    def solve(k, carry):
        sends = []
        t_sends = []

        @pl.when(k == 0)
        def _():
            for t in range(tiles):
                cols = pl.ds(t * tile, tile)
                mmat[:, cols] = nn(coup_ref[:, cols], tile_ref[t]).astype(BF16)
                qmat[:, cols] = nt(coup_ref[:, cols], tile_ref[t]).astype(BF16)
            for copy in slot_copies:
                copy.wait()
            to_smem = pltpu.make_async_copy(slot_v, slot_s, slot_sem)
            to_smem.start()
            to_smem.wait()

        @pl.when(k > 0)
        def _():
            for t in range(tiles):
                cols = pl.ds(t * tile, tile)
                leaf = solved[:, cols] - nn(picked[...], qmat[:, cols])
                x = rhs_ref[:, cols].astype(F32) - scale_ref[:, cols] * leaf
                solved[:, cols] = nt(x.astype(BF16), tile_ref[t])

        r_copies = []
        for g in n_groups:
            tbuf, rsend, rrecv = buffers[g][0], buffers[g][1], buffers[g][2]
            copies = touched_first(g, k)
            cores = [copies[-1]]
            for j in range(1, n_z):
                copies[j - 1].wait_recv()
                piece = tbuf.at[k, on_z(j, c), pl.ds(0, pb)]
                cores += started([to_core(piece, sems[g][2], sems[g][3], j)])
            for copy in cores:
                copy.wait_recv()
            t_sends += copies[:-1] + cores
            for a in range(n_sec):
                for j in range(per):
                    q = a * per_sec + d * per + j
                    total = tbuf[k, 0, slot_s[0, 0, q]].astype(F32)
                    for i in range(1, n_dev):
                        total = total + tbuf[k, i, slot_s[i, 0, q]].astype(F32)
                    rsend[k, a, j] = total.astype(BF16)
            r_copies.append(started([
                remote(rsend.at[k, (s + j) % n_sec], sems[g][4].at[j], sems[g][5].at[j],
                       {"sec": (s + j) % n_sec}, rrecv.at[k, s])
                for j in range(1, n_sec)
            ]))
            sends += r_copies[g]

        def rhs_first(g):
            mine = buffers[g][3].at[k, d]
            return (along_z(mine, sems[g][6], sems[g][7])
                    + [to_core(mine, sems[g][8], sems[g][9], 0)])

        h_copies = []
        for g in n_groups:
            _, rsend, rrecv, hbuf, _, _, link = buffers[g]
            totals = []
            for j in range(per):
                prev = link[k, own_rhs + j].astype(F32)
                totals.append(-lscale_ref[pl.ds(own_rhs + j, 1), :] * prev
                              - rsend[k, s, j].astype(F32))
            for copy in r_copies[g]:
                copy.wait_recv()
            for j in range(per):
                total = totals[j]
                for i in range(1, n_sec):
                    total = total - rrecv[k, (s + i) % n_sec, j].astype(F32)
                hbuf[k, d, j] = total.astype(BF16)
            h_copies.append(started(rhs_first(g)))

        @pl.when(k == 0)
        def _():
            linv_load.wait()

        def multiply(g, owner):
            hbuf = buffers[g][3]
            left = jnp.concatenate([hbuf[k, owner, j] for j in range(per)], axis=1)
            depth = per * panel
            return nn(left, linv[pl.ds(pl.multiple_of(owner * depth, depth), depth), :])

        for g in n_groups:
            part[rows(g), :] = multiply(g, d)

        @pl.when(k < SOLVES - 1)
        def _():
            total = base[...]
            for t in range(tiles):
                cols = pl.ds(t * tile, tile)
                scaled = (scale_ref[:, cols] * solved[:, cols]).astype(BF16)
                total = total - nt(scaled, mmat[:, cols])
            umat[...] = total

        l_copies = []
        for g in n_groups:
            hbuf, lsend, lrecv = buffers[g][3], buffers[g][4], buffers[g][5]
            copies = h_copies[g]
            cores = [copies[-1]]
            for j in range(1, n_z):
                copies[j - 1].wait_recv()
                owner = on_z(j, c)
                cores += started([to_core(hbuf.at[k, owner], sems[g][8], sems[g][9], j)])
                part[rows(g), :] += multiply(g, owner)
            for j in range(n_z):
                cores[j].wait_recv()
                part[rows(g), :] += multiply(g, on_z(j, 1 - c))
            sends += copies[:-1] + cores
            for q in range(per_dev):
                lsend[k, q] = part[rows(g), q * panel:(q + 1) * panel].astype(BF16)
            l_copies.append(started([
                remote(lsend.at[k, pl.ds(((s + j) % n_sec) * per, per)],
                       sems[g][10].at[j], sems[g][11].at[j],
                       {"sec": (s + j) % n_sec}, lrecv.at[k, s])
                for j in range(1, n_sec)
            ]))
            sends += l_copies[g]

        @pl.when(k == 0)
        def _():
            for t in range(tiles):
                cols = pl.ds(t * tile, tile)
                scaled = (scale_ref[:, cols] * qmat[:, cols].astype(F32)).astype(BF16)
                term = nt(scaled, mmat[:, cols])
                if t == 0:
                    kacc[...] = term
                else:
                    kacc[...] += term
            kmat[...] = kacc[...].astype(BF16)

        def piece(g, owner, section):
            return buffers[g][6].at[k + 1, pl.ds(owner * per_dev + section * per, per)]

        z_copies = []
        for g in n_groups:
            lrecv, link = buffers[g][5], buffers[g][6]
            for copy in l_copies[g]:
                copy.wait_recv()
            for j in range(per):
                own_cols = pl.ds(pl.multiple_of((s * per + j) * panel, panel), panel)
                total = part[rows(g), own_cols]
                for i in range(1, n_sec):
                    total = total + lrecv[k, (s + i) % n_sec, j].astype(F32)
                link[k + 1, d * per_dev + s * per + j] = total.astype(BF16)
            z_copies.append(started(along_z(piece(g, d, s), sems[g][12], sems[g][13])))
            sends += z_copies[g]
        g_copies = []
        for g in n_groups:
            g_copies.append([])
            for i in range(n_z):
                if i > 0:
                    z_copies[g][i - 1].wait_recv()
                g_copies[g].append(started([
                    remote(piece(g, on_z(i, c), s), sems[g][14].at[i, j], sems[g][15].at[i, j],
                           {"sec": (s + j) % n_sec})
                    for j in range(1, n_sec)
                ]))
                sends += g_copies[g][i]
        c_copies = []
        for g in n_groups:
            c_copies.append([])
            for i in range(n_z):
                for copy in g_copies[g][i]:
                    copy.wait_recv()
                whole = buffers[g][6].at[k + 1, pl.ds(on_z(i, c) * per_dev, per_dev)]
                c_copies[g] += started([to_core(whole, sems[g][16], sems[g][17], i)])
            sends += c_copies[g]
        for copy in t_sends:
            copy.wait_send()
        for g in n_groups:
            for copy in c_copies[g]:
                copy.wait_recv()
            for q in range(pb):
                picked[rows(g), q * panel:(q + 1) * panel] = buffers[g][6][k + 1, panels_ref[0, q]]

            @pl.when(k < SOLVES - 1)
            def _():
                store_touched(g, k + 1, umat[rows(g), :] + nn(picked[rows(g), :], kmat[...]))

        for copy in sends:
            copy.wait_send()
        return carry

    lax.fori_loop(0, SOLVES, solve, 0)

    for t in range(tiles):
        cols = pl.ds(t * tile, tile)
        leaf_out[:, cols] = (solved[:, cols] - nn(picked[...], qmat[:, cols])).astype(BF16)
    for g in n_groups:
        for q in range(per_dev):
            link_out[rows(g), q * panel:(q + 1) * panel] = buffers[g][6][SOLVES, d * per_dev + q]


def row_groups(cols):
    if cols % 16 or cols < 32:
        return ((0, cols),)
    first = (cols // 16 + 1) // 2 * 16
    return ((0, first), (first, cols - first))


def fused(n_sec, n_dev, per, tile_inverse, link_coupling, link_panels, leaf_rhs, leaf_scale,
          link_scale, link_inverse):
    pb = link_panels.shape[1]
    rows, nb = link_coupling.shape[1:]
    panel = rows // pb
    cols = leaf_rhs.shape[1]
    total_panels = link_scale.shape[0] // panel
    per_dev = n_sec * per
    n_z = n_dev // 2
    groups = row_groups(cols)
    vmem = pl.BlockSpec(memory_space=pltpu.VMEM)
    dma = pltpu.SemaphoreType.DMA
    scratch = [
        pltpu.VMEM(tile_inverse.shape[1:], BF16),
        pltpu.VMEM((rows, nb), BF16),
        pltpu.VMEM((cols, nb), BF16),
        pltpu.VMEM((1, nb), F32),
        pltpu.VMEM((total_panels, panel), F32),
        pltpu.VMEM(link_inverse.shape, BF16),
        pltpu.VMEM((n_dev, 8, 128), jnp.int32),
        pltpu.SMEM((n_dev, 8, 128), jnp.int32),
        pltpu.VMEM((rows, nb), BF16),
        pltpu.VMEM((rows, nb), BF16),
        pltpu.VMEM((rows, rows), BF16),
        pltpu.VMEM((rows, rows), F32),
        pltpu.VMEM((cols, rows), F32),
        pltpu.VMEM((cols, nb), F32),
        pltpu.VMEM((cols, rows), F32),
        pltpu.VMEM((cols, rows), BF16),
        pltpu.VMEM((cols, per_dev * panel), F32),
        dma((tile_inverse.shape[1] + 5,)), dma, dma((n_dev,)), dma((n_dev,)),
    ]
    for _, size in groups:
        scratch += [
            pltpu.VMEM((SOLVES, n_dev, pb + 1, size, panel), BF16),
            pltpu.VMEM((SOLVES, n_sec, per, size, panel), BF16),
            pltpu.VMEM((SOLVES, n_sec, per, size, panel), BF16),
            pltpu.VMEM((SOLVES, n_dev, per, size, panel), BF16),
            pltpu.VMEM((SOLVES, per_dev, size, panel), BF16),
            pltpu.VMEM((SOLVES, n_sec, per, size, panel), BF16),
            pltpu.VMEM((SOLVES + 1, total_panels, size, panel), BF16),
        ]
        for shape in ((n_z,), (n_z,), (n_sec,), (n_z,), (n_z,), (n_sec,), (n_z,),
                      (n_z, n_sec), (n_z,)):
            scratch += [dma(shape), dma(shape)]
    leaf, link = pl.pallas_call(
        functools.partial(kernel, n_sec, n_dev, per, groups),
        out_shape=(
            jax.ShapeDtypeStruct((cols, nb), BF16),
            jax.ShapeDtypeStruct((cols, per_dev * panel), BF16),
        ),
        in_specs=[pl.BlockSpec(memory_space=pltpu.SMEM)]
        + [pl.BlockSpec(memory_space=pl.ANY)] * 6,
        out_specs=(vmem, vmem),
        scratch_shapes=scratch,
        compiler_params=pltpu.CompilerParams(
            collective_id=0, has_side_effects=True, vmem_limit_bytes=56 * 1024 * 1024
        ),
    )(
        link_panels, tile_inverse[0], link_coupling[0], leaf_rhs[0], leaf_scale,
        link_scale.reshape(total_panels, panel), link_inverse,
    )
    return leaf[None], link


def apply_tiles(tile_inv, vectors):
    columns = vectors.shape[0]
    blocked = vectors.reshape(columns, tile_inv.shape[0], tile_inv.shape[1])
    result = jnp.einsum("tab,ctb->cta", tile_inv, blocked, preferred_element_type=F32)
    return result.reshape(columns, -1)


def plain(tile_inverse, link_coupling, link_panels, leaf_rhs, leaf_scale, link_scale, link_inverse):
    tile_inv, coupling, leaf_gain = tile_inverse[0], link_coupling[0], leaf_scale[0]
    own_panels = link_panels[0]
    pb = own_panels.shape[0]
    panel = coupling.shape[0] // pb
    link_size = link_scale.shape[0]
    panel_count = link_size // panel
    matches = own_panels[:, None] == jnp.arange(panel_count, dtype=jnp.int32)[None, :]
    selector = matches.astype(BF16)
    spreader = matches.astype(F32)
    columns = leaf_rhs.shape[1]
    previous = jnp.zeros(leaf_rhs.shape[1:], BF16)
    linking = jnp.zeros((columns, link_size), BF16)
    for solve_index in range(SOLVES):
        corrected = leaf_rhs[0].astype(F32) - leaf_gain[None, :] * previous.astype(F32)
        corrected = corrected.astype(BF16)
        link_side = -link_scale[None, :] * linking.astype(F32)
        solved = apply_tiles(tile_inv, corrected).astype(BF16)
        touched = jnp.einsum("cn,rn->cr", solved, coupling, preferred_element_type=F32)
        touched = touched.reshape(columns, pb, panel)
        spread = jnp.einsum("csr,sq->cqr", touched, spreader).reshape(columns, link_size)
        section = lax.psum_scatter(
            spread.astype(BF16), "sec", scatter_dimension=1, tiled=True
        ).astype(F32)
        summed = lax.psum(section, "dev")
        width = summed.shape[1]
        own_slab = lax.dynamic_slice_in_dim(link_side, lax.axis_index("sec") * width, width, 1)
        link_rhs = (own_slab - summed).astype(BF16)
        partial_value = jnp.dot(link_rhs, link_inverse, preferred_element_type=F32)
        own_part = lax.psum(partial_value, "sec").astype(BF16)
        linking = lax.all_gather(own_part, "dev", axis=1, tiled=True)
        picked = jnp.einsum(
            "cqr,sq->csr", linking.reshape(columns, panel_count, panel), selector,
            preferred_element_type=F32,
        )
        picked = picked.reshape(columns, pb * panel).astype(BF16)
        pushed = jnp.dot(picked, coupling, preferred_element_type=F32)
        reduced = (corrected.astype(F32) - pushed).astype(BF16)
        previous = apply_tiles(tile_inv, reduced).astype(BF16)
    width = link_size // lax.axis_size("dev")
    link_out = lax.dynamic_slice_in_dim(linking, lax.axis_index("dev") * width, width, 1)
    return previous[None], link_out


def per_device(n_sec, n_dev, *args):
    link_coupling, link_panels, link_scale = args[1], args[2], args[5]
    panel = link_coupling.shape[1] // link_panels.shape[1]
    panels = link_scale.shape[0] // panel
    fits = n_dev % 2 == 0 and panels % (n_sec * n_dev) == 0 and panels <= 128
    if fits and n_sec > 1 and link_coupling.shape[0] == 1:
        return fused(n_sec, n_dev, panels // (n_sec * n_dev), *args)
    return plain(*args)


def solution(mesh):
    in_specs = (
        P(("sec", "dev"), None, None, None),
        P(("sec", "dev"), None, None),
        P(("sec", "dev"), None),
        P(("sec", "dev"), None, None),
        P(("sec", "dev"), None),
        P(),
        P("sec", "dev"),
    )
    out_specs = (P(("sec", "dev"), None, None), P(None, "dev"))
    body = functools.partial(per_device, mesh.shape["sec"], mesh.shape["dev"])
    return jax.shard_map(
        body, mesh=mesh, in_specs=in_specs, out_specs=out_specs, check_vma=False
    )
```

time: 175 us -> 147 us (0.84)
  Pallas kernels: 166 us -> 143 us
  local copies, waits for them, and re-layouts: 7.54 us -> 3.16 us
    pallas_call x1, Pallas kernels: 166 us -> 143 us  [fused(): pl.pallas_call(functools.partial(kernel, n_sec, n_dev, per, groups), out_...]
    unnamed x14 -> x2, local copies, waits for them, and re-layouts: 7.53 us -> 3.16 us
where the time goes in v2:
time: 147 us
  Pallas kernels  143 us (97%)
  local copies, waits for them, and re-layouts  3.16 us (2%)
    pallas_call x1, Pallas kernels, fused(): pl.pallas_call(functools.partial(kernel, n_sec, n_dev, per, groups), out_...  143 us
    unnamed x2, local copies, waits for them, and re-layouts  3.16 us

profile of v2, /device:TPU:0, one launch (start us, length us, event | category | flops | bytes accessed | tf_op | source)
XLA Modules:
  0.0 147.1 jit_solution(17433444859326957747)
XLA Ops:
  0.6 143.3 %shard_map.86 = (bf16[48,2048]{1,0:T(8,128)(2,1)}, bf16[48,1024]{1,0:T(8,128)(2,1)}) custom-call(s32[1,4]{1,0:T(1,128)} %refs_0_.1, bf16[4,512,512]{2,1,0:T(8,128)(2,1)} %bitcast.5, bf16[512,2048]{1,0:T(8,128)(2,1)} %bitcast.6, bf16[48,2048]{1,0:T(8,128)(2,1)} %bitcast.8, f32[1,2048]{1,0:T(1,128)} %refs_4_.1, f32[64,128]{1,0:T(8,128)} %bitcast.9, ...), custom_call_target="tpu_custom_call" | custom-call | tf_op jit(solution)/shard_map/pallas_call | solution.py:392
  143.9 1.6 %copy.11 = bf16[1,48,2048]{2,1,0:T(8,128)(2,1)} copy(bf16[1,48,2048]{2,1,0:T(8,128)(2,1)} %bitcast.7) | data formatting | bytes 393216
  145.6 1.5 %copy.12 = bf16[48,1024]{1,0:T(8,128)(2,1)} copy(bf16[48,1024]{1,0:T(8,128)(2,1)} %get-tuple-element.9) | data formatting | bytes 196608

commit v3 on v2

--- a/solution.py
+++ b/solution.py
@@ -21,16 +21,16 @@
 
 
 PER_GROUP = 7
-SEMS = 18
+SEMS = 14
 
 
 def kernel(n_sec, n_dev, per, groups, *refs):
     (panels_ref, tile_hbm, coup_hbm, rhs_hbm, scale_hbm, lscale_hbm, linv_hbm,
      leaf_out, link_out,
-     tile_ref, coup_ref, rhs_ref, scale_ref, lscale_ref, linv, slot_v, slot_s,
+     tile_ref, coup_ref, rhs_ref, scale_ref, lscale_ref, wown, wother, slot_v, slot_s,
      mmat, qmat, kmat, kacc, base, solved, umat, picked, part,
-     in_sem, slot_sem, slot_send, slot_recv) = refs[:30]
-    rest = refs[30:]
+     in_sem, slot_sem, slot_send, slot_recv, w_send, w_recv) = refs[:33]
+    rest = refs[33:]
     span = PER_GROUP + SEMS
     buffers = [rest[g * span:g * span + PER_GROUP] for g in range(len(groups))]
     sems = [rest[g * span + PER_GROUP:(g + 1) * span] for g in range(len(groups))]
@@ -78,21 +78,30 @@
     tile_loads = [load(tile_hbm.at[t], tile_ref.at[t]) for t in range(tiles)]
     scale_load = load(scale_hbm, scale_ref)
     lscale_load = load(lscale_hbm, lscale_ref)
-    linv_load = load(linv_hbm, linv)
+
+    def inverse_rows(owner):
+        depth = per * panel
+        return linv_hbm.at[pl.ds(pl.multiple_of(owner * depth, depth), depth)]
+
+    w_loads = [load(inverse_rows(i * 2 + c), wown.at[i]) for i in range(n_z)]
 
     barrier = pltpu.get_barrier_semaphore()
-    for j in range(1, n_dev):
-        pl.semaphore_signal(barrier, inc=1, device_id={"dev": (d + j) % n_dev},
+    def at_z(m):
+        return {"sec": (s + m // 2) % n_sec, "dev": z * 2 + (c + m % 2) % 2}
+
+    n_at_z = 2 * n_sec
+    for j in range(1, n_z):
+        pl.semaphore_signal(barrier, inc=1, device_id={"dev": on_z(j, c)},
                             device_id_type=pl.DeviceIdType.MESH)
-    for j in range(1, n_sec):
-        pl.semaphore_signal(barrier, inc=1, device_id={"sec": (s + j) % n_sec},
+    for m in range(1, n_at_z):
+        pl.semaphore_signal(barrier, inc=1, device_id=at_z(m),
                             device_id_type=pl.DeviceIdType.MESH)
 
     for g in n_groups:
         tbuf, link = buffers[g][0], buffers[g][6]
         zero_panel = jnp.zeros(tbuf.shape[3:], BF16)
         for k in range(SOLVES):
-            for i in range(n_dev):
+            for i in range(n_z):
                 tbuf[k, i, pb] = zero_panel
         for j in range(per):
             link[0, own_rhs + j] = zero_panel
@@ -100,7 +109,7 @@
     slots = jnp.full(slot_v.shape[1:], pb, jnp.int32)
     for q in range(pb):
         slots = jnp.where(lane == panels_ref[0, q], q, slots)
-    slot_v[d] = slots
+    slot_v[z] = slots
 
     rhs_load.wait()
     first = None
@@ -115,12 +124,7 @@
         first = term if first is None else first + term
     base[...] = first
 
-    pl.semaphore_wait(barrier, n_dev - 1 + n_sec - 1)
-
-    slot_copies = started([
-        remote(slot_v.at[d], slot_send.at[j], slot_recv.at[j], {"dev": (d + j) % n_dev})
-        for j in range(1, n_dev)
-    ])
+    pl.semaphore_wait(barrier, n_z - 1 + n_at_z - 1)
 
     def along_z(ref, send, recv):
         return [remote(ref, send.at[j], recv.at[j], {"dev": ((z + j) % n_z) * 2 + c})
@@ -129,18 +133,22 @@
     def to_core(ref, send, recv, j):
         return remote(ref, send.at[j], recv.at[j], {"dev": partner})
 
-    def touched_first(g, k):
-        mine = buffers[g][0].at[k, d, pl.ds(0, pb)]
-        return (along_z(mine, sems[g][0], sems[g][1])
-                + [to_core(mine, sems[g][2], sems[g][3], 0)])
+    def touched_sends(g, k):
+        return along_z(buffers[g][0].at[k, z, pl.ds(0, pb)], sems[g][0], sems[g][1])
 
     def store_touched(g, k, value):
         for q in range(pb):
-            buffers[g][0][k, d, q] = value[:, q * panel:(q + 1) * panel].astype(BF16)
-        started(touched_first(g, k))
+            buffers[g][0][k, z, q] = value[:, q * panel:(q + 1) * panel].astype(BF16)
+        started(touched_sends(g, k))
 
     for g in n_groups:
         store_touched(g, 0, base[rows(g), :])
+    slot_copies = started(along_z(slot_v.at[z], slot_send, slot_recv))
+    w_copies = started([
+        remote(inverse_rows(i * 2 + 1 - c), w_send.at[i], w_recv.at[i], {"dev": partner},
+               wother.at[i])
+        for i in range(n_z)
+    ])
     scale_load.wait()
     lscale_load.wait()
 
@@ -171,33 +179,24 @@
         r_copies = []
         for g in n_groups:
             tbuf, rsend, rrecv = buffers[g][0], buffers[g][1], buffers[g][2]
-            copies = touched_first(g, k)
-            cores = [copies[-1]]
-            for j in range(1, n_z):
-                copies[j - 1].wait_recv()
-                piece = tbuf.at[k, on_z(j, c), pl.ds(0, pb)]
-                cores += started([to_core(piece, sems[g][2], sems[g][3], j)])
-            for copy in cores:
+            copies = touched_sends(g, k)
+            for copy in copies:
                 copy.wait_recv()
-            t_sends += copies[:-1] + cores
+            t_sends += copies
             for a in range(n_sec):
-                for j in range(per):
-                    q = a * per_sec + d * per + j
-                    total = tbuf[k, 0, slot_s[0, 0, q]].astype(F32)
-                    for i in range(1, n_dev):
-                        total = total + tbuf[k, i, slot_s[i, 0, q]].astype(F32)
-                    rsend[k, a, j] = total.astype(BF16)
+                for b in range(2):
+                    for j in range(per):
+                        q = a * per_sec + (z * 2 + b) * per + j
+                        total = tbuf[k, 0, slot_s[0, 0, q]].astype(F32)
+                        for i in range(1, n_z):
+                            total = total + tbuf[k, i, slot_s[i, 0, q]].astype(F32)
+                        rsend[k, a, b, j] = total.astype(BF16)
             r_copies.append(started([
-                remote(rsend.at[k, (s + j) % n_sec], sems[g][4].at[j], sems[g][5].at[j],
-                       {"sec": (s + j) % n_sec}, rrecv.at[k, s])
-                for j in range(1, n_sec)
+                remote(rsend.at[k, (s + m // 2) % n_sec, (c + m % 2) % 2], sems[g][2].at[m],
+                       sems[g][3].at[m], at_z(m), rrecv.at[k, m])
+                for m in range(1, n_at_z)
             ]))
             sends += r_copies[g]
-
-        def rhs_first(g):
-            mine = buffers[g][3].at[k, d]
-            return (along_z(mine, sems[g][6], sems[g][7])
-                    + [to_core(mine, sems[g][8], sems[g][9], 0)])
 
         h_copies = []
         for g in n_groups:
@@ -206,28 +205,30 @@
             for j in range(per):
                 prev = link[k, own_rhs + j].astype(F32)
                 totals.append(-lscale_ref[pl.ds(own_rhs + j, 1), :] * prev
-                              - rsend[k, s, j].astype(F32))
+                              - rsend[k, s, c, j].astype(F32))
             for copy in r_copies[g]:
                 copy.wait_recv()
             for j in range(per):
                 total = totals[j]
-                for i in range(1, n_sec):
-                    total = total - rrecv[k, (s + i) % n_sec, j].astype(F32)
-                hbuf[k, d, j] = total.astype(BF16)
-            h_copies.append(started(rhs_first(g)))
+                for m in range(1, n_at_z):
+                    total = total - rrecv[k, m, j].astype(F32)
+                hbuf[k, z, j] = total.astype(BF16)
+            h_copies.append(started(along_z(hbuf.at[k, z], sems[g][4], sems[g][5])))
 
         @pl.when(k == 0)
         def _():
-            linv_load.wait()
+            for copy in w_loads + w_copies:
+                copy.wait()
 
         def multiply(g, owner):
             hbuf = buffers[g][3]
             left = jnp.concatenate([hbuf[k, owner, j] for j in range(per)], axis=1)
-            depth = per * panel
-            return nn(left, linv[pl.ds(pl.multiple_of(owner * depth, depth), depth), :])
-
-        for g in n_groups:
-            part[rows(g), :] = multiply(g, d)
+            return nn(left, wown[owner]), nn(left, wother[owner])
+
+        half = per_dev * panel
+
+        for g in n_groups:
+            part[rows(g), :half], part[rows(g), half:] = multiply(g, z)
 
         @pl.when(k < SOLVES - 1)
         def _():
@@ -242,23 +243,20 @@
         for g in n_groups:
             hbuf, lsend, lrecv = buffers[g][3], buffers[g][4], buffers[g][5]
             copies = h_copies[g]
-            cores = [copies[-1]]
             for j in range(1, n_z):
                 copies[j - 1].wait_recv()
-                owner = on_z(j, c)
-                cores += started([to_core(hbuf.at[k, owner], sems[g][8], sems[g][9], j)])
-                part[rows(g), :] += multiply(g, owner)
-            for j in range(n_z):
-                cores[j].wait_recv()
-                part[rows(g), :] += multiply(g, on_z(j, 1 - c))
-            sends += copies[:-1] + cores
-            for q in range(per_dev):
-                lsend[k, q] = part[rows(g), q * panel:(q + 1) * panel].astype(BF16)
+                near, far = multiply(g, (z - j + n_z) % n_z)
+                part[rows(g), :half] += near
+                part[rows(g), half:] += far
+            sends += copies
+            for b in range(2):
+                for q in range(per_dev):
+                    at = b * half + q * panel
+                    lsend[k, b, q] = part[rows(g), at:at + panel].astype(BF16)
             l_copies.append(started([
-                remote(lsend.at[k, pl.ds(((s + j) % n_sec) * per, per)],
-                       sems[g][10].at[j], sems[g][11].at[j],
-                       {"sec": (s + j) % n_sec}, lrecv.at[k, s])
-                for j in range(1, n_sec)
+                remote(lsend.at[k, m % 2, pl.ds(((s + m // 2) % n_sec) * per, per)],
+                       sems[g][6].at[m], sems[g][7].at[m], at_z(m), lrecv.at[k, m])
+                for m in range(1, n_at_z)
             ]))
             sends += l_copies[g]
 
@@ -285,10 +283,10 @@
             for j in range(per):
                 own_cols = pl.ds(pl.multiple_of((s * per + j) * panel, panel), panel)
                 total = part[rows(g), own_cols]
-                for i in range(1, n_sec):
-                    total = total + lrecv[k, (s + i) % n_sec, j].astype(F32)
+                for m in range(1, n_at_z):
+                    total = total + lrecv[k, m, j].astype(F32)
                 link[k + 1, d * per_dev + s * per + j] = total.astype(BF16)
-            z_copies.append(started(along_z(piece(g, d, s), sems[g][12], sems[g][13])))
+            z_copies.append(started(along_z(piece(g, d, s), sems[g][8], sems[g][9])))
             sends += z_copies[g]
         g_copies = []
         for g in n_groups:
@@ -297,7 +295,7 @@
                 if i > 0:
                     z_copies[g][i - 1].wait_recv()
                 g_copies[g].append(started([
-                    remote(piece(g, on_z(i, c), s), sems[g][14].at[i, j], sems[g][15].at[i, j],
+                    remote(piece(g, on_z(i, c), s), sems[g][10].at[i, j], sems[g][11].at[i, j],
                            {"sec": (s + j) % n_sec})
                     for j in range(1, n_sec)
                 ]))
@@ -309,7 +307,7 @@
                 for copy in g_copies[g][i]:
                     copy.wait_recv()
                 whole = buffers[g][6].at[k + 1, pl.ds(on_z(i, c) * per_dev, per_dev)]
-                c_copies[g] += started([to_core(whole, sems[g][16], sems[g][17], i)])
+                c_copies[g] += started([to_core(whole, sems[g][12], sems[g][13], i)])
             sends += c_copies[g]
         for copy in t_sends:
             copy.wait_send()
@@ -362,9 +360,10 @@
         pltpu.VMEM((cols, nb), BF16),
         pltpu.VMEM((1, nb), F32),
         pltpu.VMEM((total_panels, panel), F32),
-        pltpu.VMEM(link_inverse.shape, BF16),
-        pltpu.VMEM((n_dev, 8, 128), jnp.int32),
-        pltpu.SMEM((n_dev, 8, 128), jnp.int32),
+        pltpu.VMEM((n_z, per * panel, per_dev * panel), BF16),
+        pltpu.VMEM((n_z, per * panel, per_dev * panel), BF16),
+        pltpu.VMEM((n_z, 8, 128), jnp.int32),
+        pltpu.SMEM((n_z, 8, 128), jnp.int32),
         pltpu.VMEM((rows, nb), BF16),
         pltpu.VMEM((rows, nb), BF16),
         pltpu.VMEM((rows, rows), BF16),
@@ -373,21 +372,21 @@
         pltpu.VMEM((cols, nb), F32),
         pltpu.VMEM((cols, rows), F32),
         pltpu.VMEM((cols, rows), BF16),
-        pltpu.VMEM((cols, per_dev * panel), F32),
-        dma((tile_inverse.shape[1] + 5,)), dma, dma((n_dev,)), dma((n_dev,)),
+        pltpu.VMEM((cols, 2 * per_dev * panel), F32),
+        dma((tile_inverse.shape[1] + 4 + n_z,)), dma, dma((n_z,)), dma((n_z,)),
+        dma((n_z,)), dma((n_z,)),
     ]
     for _, size in groups:
         scratch += [
-            pltpu.VMEM((SOLVES, n_dev, pb + 1, size, panel), BF16),
-            pltpu.VMEM((SOLVES, n_sec, per, size, panel), BF16),
-            pltpu.VMEM((SOLVES, n_sec, per, size, panel), BF16),
-            pltpu.VMEM((SOLVES, n_dev, per, size, panel), BF16),
-            pltpu.VMEM((SOLVES, per_dev, size, panel), BF16),
-            pltpu.VMEM((SOLVES, n_sec, per, size, panel), BF16),
+            pltpu.VMEM((SOLVES, n_z, pb + 1, size, panel), BF16),
+            pltpu.VMEM((SOLVES, n_sec, 2, per, size, panel), BF16),
+            pltpu.VMEM((SOLVES, 2 * n_sec, per, size, panel), BF16),
+            pltpu.VMEM((SOLVES, n_z, per, size, panel), BF16),
+            pltpu.VMEM((SOLVES, 2, per_dev, size, panel), BF16),
+            pltpu.VMEM((SOLVES, 2 * n_sec, per, size, panel), BF16),
             pltpu.VMEM((SOLVES + 1, total_panels, size, panel), BF16),
         ]
-        for shape in ((n_z,), (n_z,), (n_sec,), (n_z,), (n_z,), (n_sec,), (n_z,),
-                      (n_z, n_sec), (n_z,)):
+        for shape in ((n_z,), (2 * n_sec,), (n_z,), (2 * n_sec,), (n_z,), (n_z, n_sec), (n_z,)):
             scratch += [dma(shape), dma(shape)]
     leaf, link = pl.pallas_call(
         functools.partial(kernel, n_sec, n_dev, per, groups),

time: 147 us -> 148 us (level)
  no operation moved by 1% of the time
where the time goes in v3:
time: 148 us
  Pallas kernels  144 us (97%)
  local copies, waits for them, and re-layouts  3.16 us (2%)
    pallas_call x1, Pallas kernels, fused(): pl.pallas_call(functools.partial(kernel, n_sec, n_dev, per, groups), out_...  144 us
    unnamed x2, local copies, waits for them, and re-layouts  3.16 us

profile of v3, /device:TPU:0, one launch (start us, length us, event | category | flops | bytes accessed | tf_op | source)
XLA Modules:
  0.0 147.7 jit_solution(9490669884253465065)
XLA Ops:
  0.6 143.9 %shard_map.86 = (bf16[48,2048]{1,0:T(8,128)(2,1)}, bf16[48,1024]{1,0:T(8,128)(2,1)}) custom-call(s32[1,4]{1,0:T(1,128)} %refs_0_.1, bf16[4,512,512]{2,1,0:T(8,128)(2,1)} %bitcast.5, bf16[512,2048]{1,0:T(8,128)(2,1)} %bitcast.6, bf16[48,2048]{1,0:T(8,128)(2,1)} %bitcast.8, f32[1,2048]{1,0:T(1,128)} %refs_4_.1, f32[64,128]{1,0:T(8,128)} %bitcast.9, ...), custom_call_target="tpu_custom_call" | custom-call | tf_op jit(solution)/shard_map/pallas_call | solution.py:391
  144.5 1.6 %copy.11 = bf16[1,48,2048]{2,1,0:T(8,128)(2,1)} copy(bf16[1,48,2048]{2,1,0:T(8,128)(2,1)} %bitcast.7) | data formatting | bytes 393216
  146.1 1.5 %copy.12 = bf16[48,1024]{1,0:T(8,128)(2,1)} copy(bf16[48,1024]{1,0:T(8,128)(2,1)} %get-tuple-element.9) | data formatting | bytes 196608

commit v4 on v3

--- a/solution.py
+++ b/solution.py
@@ -28,9 +28,9 @@
     (panels_ref, tile_hbm, coup_hbm, rhs_hbm, scale_hbm, lscale_hbm, linv_hbm,
      leaf_out, link_out,
      tile_ref, coup_ref, rhs_ref, scale_ref, lscale_ref, wown, wother, slot_v, slot_s,
-     mmat, qmat, kmat, kacc, base, solved, umat, picked, part,
-     in_sem, slot_sem, slot_send, slot_recv, w_send, w_recv) = refs[:33]
-    rest = refs[33:]
+     tile_t, mmat, qmat, kmat, kacc, base, solved, umat, picked, part,
+     in_sem, slot_sem, slot_send, slot_recv, w_send, w_recv) = refs[:34]
+    rest = refs[34:]
     span = PER_GROUP + SEMS
     buffers = [rest[g * span:g * span + PER_GROUP] for g in range(len(groups))]
     sems = [rest[g * span + PER_GROUP:(g + 1) * span] for g in range(len(groups))]
@@ -116,7 +116,8 @@
     for t in range(tiles):
         cols = pl.ds(t * tile, tile)
         tile_loads[t].wait()
-        value = nt(rhs_ref[:, cols], tile_ref[t])
+        tile_t[t] = tile_ref[t].T
+        value = nn(rhs_ref[:, cols], tile_t[t])
         solved[:, cols] = value
         if t == 0:
             coup_load.wait()
@@ -160,8 +161,8 @@
         def _():
             for t in range(tiles):
                 cols = pl.ds(t * tile, tile)
-                mmat[:, cols] = nn(coup_ref[:, cols], tile_ref[t]).astype(BF16)
-                qmat[:, cols] = nt(coup_ref[:, cols], tile_ref[t]).astype(BF16)
+                mmat[cols, :] = nn(coup_ref[:, cols], tile_ref[t]).astype(BF16).T
+                qmat[:, cols] = nn(coup_ref[:, cols], tile_t[t]).astype(BF16)
             for copy in slot_copies:
                 copy.wait()
             to_smem = pltpu.make_async_copy(slot_v, slot_s, slot_sem)
@@ -174,7 +175,7 @@
                 cols = pl.ds(t * tile, tile)
                 leaf = solved[:, cols] - nn(picked[...], qmat[:, cols])
                 x = rhs_ref[:, cols].astype(F32) - scale_ref[:, cols] * leaf
-                solved[:, cols] = nt(x.astype(BF16), tile_ref[t])
+                solved[:, cols] = nn(x.astype(BF16), tile_t[t])
 
         r_copies = []
         for g in n_groups:
@@ -236,7 +237,7 @@
             for t in range(tiles):
                 cols = pl.ds(t * tile, tile)
                 scaled = (scale_ref[:, cols] * solved[:, cols]).astype(BF16)
-                total = total - nt(scaled, mmat[:, cols])
+                total = total - nn(scaled, mmat[cols, :])
             umat[...] = total
 
         l_copies = []
@@ -265,7 +266,7 @@
             for t in range(tiles):
                 cols = pl.ds(t * tile, tile)
                 scaled = (scale_ref[:, cols] * qmat[:, cols].astype(F32)).astype(BF16)
-                term = nt(scaled, mmat[:, cols])
+                term = nn(scaled, mmat[cols, :])
                 if t == 0:
                     kacc[...] = term
                 else:
@@ -364,7 +365,8 @@
         pltpu.VMEM((n_z, per * panel, per_dev * panel), BF16),
         pltpu.VMEM((n_z, 8, 128), jnp.int32),
         pltpu.SMEM((n_z, 8, 128), jnp.int32),
-        pltpu.VMEM((rows, nb), BF16),
+        pltpu.VMEM(tile_inverse.shape[1:], BF16),
+        pltpu.VMEM((nb, rows), BF16),
         pltpu.VMEM((rows, nb), BF16),
         pltpu.VMEM((rows, rows), BF16),
         pltpu.VMEM((rows, rows), F32),

time: 148 us -> 147 us (level)
  no operation moved by 1% of the time
where the time goes in v4:
time: 147 us
  Pallas kernels  143 us (97%)
  local copies, waits for them, and re-layouts  3.16 us (2%)
    pallas_call x1, Pallas kernels, fused(): pl.pallas_call(functools.partial(kernel, n_sec, n_dev, per, groups), out_...  143 us
    unnamed x2, local copies, waits for them, and re-layouts  3.16 us

profile of v4, /device:TPU:0, one launch (start us, length us, event | category | flops | bytes accessed | tf_op | source)
XLA Modules:
  0.0 147.1 jit_solution(9216623947446817836)
XLA Ops:
  0.6 143.3 %shard_map.86 = (bf16[48,2048]{1,0:T(8,128)(2,1)}, bf16[48,1024]{1,0:T(8,128)(2,1)}) custom-call(s32[1,4]{1,0:T(1,128)} %refs_0_.1, bf16[4,512,512]{2,1,0:T(8,128)(2,1)} %bitcast.5, bf16[512,2048]{1,0:T(8,128)(2,1)} %bitcast.6, bf16[48,2048]{1,0:T(8,128)(2,1)} %bitcast.8, f32[1,2048]{1,0:T(1,128)} %refs_4_.1, f32[64,128]{1,0:T(8,128)} %bitcast.9, ...), custom_call_target="tpu_custom_call" | custom-call | tf_op jit(solution)/shard_map/pallas_call | solution.py:393
  143.9 1.6 %copy.11 = bf16[1,48,2048]{2,1,0:T(8,128)(2,1)} copy(bf16[1,48,2048]{2,1,0:T(8,128)(2,1)} %bitcast.7) | data formatting | bytes 393216
  145.5 1.5 %copy.12 = bf16[48,1024]{1,0:T(8,128)(2,1)} copy(bf16[48,1024]{1,0:T(8,128)(2,1)} %get-tuple-element.9) | data formatting | bytes 196608

commit v5 on v4

--- a/solution.py
+++ b/solution.py
@@ -336,13 +336,6 @@
             link_out[rows(g), q * panel:(q + 1) * panel] = buffers[g][6][SOLVES, d * per_dev + q]
 
 
-def row_groups(cols):
-    if cols % 16 or cols < 32:
-        return ((0, cols),)
-    first = (cols // 16 + 1) // 2 * 16
-    return ((0, first), (first, cols - first))
-
-
 def fused(n_sec, n_dev, per, tile_inverse, link_coupling, link_panels, leaf_rhs, leaf_scale,
           link_scale, link_inverse):
     pb = link_panels.shape[1]
@@ -352,7 +345,7 @@
     total_panels = link_scale.shape[0] // panel
     per_dev = n_sec * per
     n_z = n_dev // 2
-    groups = row_groups(cols)
+    groups = ((0, cols),)
     vmem = pl.BlockSpec(memory_space=pltpu.VMEM)
     dma = pltpu.SemaphoreType.DMA
     scratch = [
@@ -401,7 +394,7 @@
         out_specs=(vmem, vmem),
         scratch_shapes=scratch,
         compiler_params=pltpu.CompilerParams(
-            collective_id=0, has_side_effects=True, vmem_limit_bytes=56 * 1024 * 1024
+            collective_id=0, has_side_effects=True, vmem_limit_bytes=48 * 1024 * 1024
         ),
     )(
         link_panels, tile_inverse[0], link_coupling[0], leaf_rhs[0], leaf_scale,

time: 147 us -> 154 us (1.048)
  local copies, waits for them, and re-layouts: 3.16 us -> 7.53 us
  Pallas kernels: 143 us -> 146 us
    unnamed x2 -> x14, local copies, waits for them, and re-layouts: 3.16 us -> 7.53 us
    pallas_call x1, Pallas kernels: 143 us -> 146 us  [fused(): pl.pallas_call(functools.partial(kernel, n_sec, n_dev, per, groups), out_...]
where the time goes in v5:
time: 154 us
  Pallas kernels  146 us (95%)
  local copies, waits for them, and re-layouts  7.53 us (5%)
    pallas_call x1, Pallas kernels, fused(): pl.pallas_call(functools.partial(kernel, n_sec, n_dev, per, groups), out_...  146 us
    unnamed x14, local copies, waits for them, and re-layouts  7.53 us

profile of v5, /device:TPU:0, one launch (start us, length us, event | category | flops | bytes accessed | tf_op | source)
XLA Modules:
  0.0 153.9 jit_solution(2761838186117567146)
XLA Ops:
  0.6 0.0 copy-start
  0.6 1.6 %copy-done = bf16[1,4,512,512]{3,2,1,0:T(8,128)(2,1)S(1)} copy-done((bf16[1,4,512,512]{3,2,1,0:T(8,128)(2,1)S(1)}, bf16[1,4,512,512]{3,2,1,0:T(8,128)(2,1)}, u32[]{:S(2)}) %copy-start) | copy-done | bytes 2097176
  2.2 0.0 copy-start.1
  2.2 1.6 %copy-done.1 = bf16[1,512,2048]{2,1,0:T(8,128)(2,1)S(1)} copy-done((bf16[1,512,2048]{2,1,0:T(8,128)(2,1)S(1)}, bf16[1,512,2048]{2,1,0:T(8,128)(2,1)}, u32[]{:S(2)}) %copy-start.1) | copy-done | bytes 2097176
  3.8 0.0 copy-start.2
  3.8 0.9 copy-done.2
  4.7 0.0 copy-start.3
  4.7 0.8 copy-done.3
  5.5 0.0 copy-start.4
  5.5 0.7 copy-done.4
  6.2 0.0 copy-start.5
  6.2 0.7 copy-done.5
  6.9 145.8 %shard_map.86 = (bf16[48,2048]{1,0:T(8,128)(2,1)S(1)}, bf16[48,1024]{1,0:T(8,128)(2,1)S(1)}) custom-call(s32[1,4]{1,0:T(1,128)S(1)} %copy-done.5, bf16[4,512,512]{2,1,0:T(8,128)(2,1)S(1)} %bitcast.5, bf16[512,2048]{1,0:T(8,128)(2,1)S(1)} %bitcast.6, bf16[48,2048]{1,0:T(8,128)(2,1)S(1)} %bitcast.8, f32[1,2048]{1,0:T(1,128)S(1)} %copy-done.4, ...), custom_call_target="tpu_custom_call" | custom-call | tf_op jit(solution)/shard_map/pallas_call | solution.py:386
  152.6 0.7 copy.11
  153.3 0.6 copy.12
Async XLA Ops:
  0.6 1.6 %copy-start = (bf16[1,4,512,512]{3,2,1,0:T(8,128)(2,1)S(1)}, bf16[1,4,512,512]{3,2,1,0:T(8,128)(2,1)}, u32[]{:S(2)}) copy-start(bf16[1,4,512,512]{3,2,1,0:T(8,128)(2,1)} %param.7) | copy-start | bytes 6291460
  2.2 1.6 %copy-start.1 = (bf16[1,512,2048]{2,1,0:T(8,128)(2,1)S(1)}, bf16[1,512,2048]{2,1,0:T(8,128)(2,1)}, u32[]{:S(2)}) copy-start(bf16[1,512,2048]{2,1,0:T(8,128)(2,1)} %param.8) | copy-start | bytes 6291460
  3.8 0.9 copy-start.2
  4.7 0.8 copy-start.3
  5.5 0.7 copy-start.4
  6.2 0.7 copy-start.5

commit v6 on v4

--- a/solution.py
+++ b/solution.py
@@ -337,10 +337,8 @@
 
 
 def row_groups(cols):
-    if cols % 16 or cols < 32:
-        return ((0, cols),)
-    first = (cols // 16 + 1) // 2 * 16
-    return ((0, first), (first, cols - first))
+    size = 16 if cols % 16 == 0 else cols
+    return tuple((start, size) for start in range(0, cols, size))
 
 
 def fused(n_sec, n_dev, per, tile_inverse, link_coupling, link_panels, leaf_rhs, leaf_scale,

time: 147 us -> 141 us (0.959)
  Pallas kernels: 143 us -> 137 us
    pallas_call x1, Pallas kernels: 143 us -> 137 us  [fused(): pl.pallas_call(functools.partial(kernel, n_sec, n_dev, per, groups), out_...]
where the time goes in v6:
time: 141 us
  Pallas kernels  137 us (97%)
  local copies, waits for them, and re-layouts  3.16 us (2%)
    pallas_call x1, Pallas kernels, fused(): pl.pallas_call(functools.partial(kernel, n_sec, n_dev, per, groups), out_...  137 us
    unnamed x2, local copies, waits for them, and re-layouts  3.16 us

profile of v6, /device:TPU:0, one launch (start us, length us, event | category | flops | bytes accessed | tf_op | source)
XLA Modules:
  0.0 140.6 jit_solution(10147723411824833273)
XLA Ops:
  0.6 136.8 %shard_map.86 = (bf16[48,2048]{1,0:T(8,128)(2,1)}, bf16[48,1024]{1,0:T(8,128)(2,1)}) custom-call(s32[1,4]{1,0:T(1,128)} %refs_0_.1, bf16[4,512,512]{2,1,0:T(8,128)(2,1)} %bitcast.5, bf16[512,2048]{1,0:T(8,128)(2,1)} %bitcast.6, bf16[48,2048]{1,0:T(8,128)(2,1)} %bitcast.8, f32[1,2048]{1,0:T(1,128)} %refs_4_.1, f32[64,128]{1,0:T(8,128)} %bitcast.9, ...), custom_call_target="tpu_custom_call" | custom-call | tf_op jit(solution)/shard_map/pallas_call | solution.py:391
  137.5 1.6 %copy.11 = bf16[1,48,2048]{2,1,0:T(8,128)(2,1)} copy(bf16[1,48,2048]{2,1,0:T(8,128)(2,1)} %bitcast.7) | data formatting | bytes 393216
  139.1 1.5 %copy.12 = bf16[48,1024]{1,0:T(8,128)(2,1)} copy(bf16[48,1024]{1,0:T(8,128)(2,1)} %get-tuple-element.9) | data formatting | bytes 196608
